TPU v7x, 768 devices: a whole 4x8x12 slice. The times are simulated.
768 devices in a mesh: rep: 48 (over z, x_lo, core), blk: 16 (over y, x_hi).
Axes of the slice: x: 4 (x_hi: 2, x_lo: 2; x = x_hi * 2 + x_lo), y: 8, z: 12, core: 2. Of those that a mesh axis runs over, the one named last changes fastest.
Arguments:
- features: bfloat16 [98304, 128], P(('rep', 'blk')), may hold values from -6 to 6
- weight: bfloat16 [128, 128], replicated, may hold values from -0.5 to 0.5
- bias: float32 [128], replicated, may hold values from -3 to 3
- tile_vals: bfloat16 [48, 16, 128, 128, 128], P('rep', 'blk'), may hold values from -0.078125 to 0.078125
- tile_pos: int32 [48, 16, 128], P('rep', 'blk'), may hold values from 0 to 47
- tile_counts: int32 [48, 16, 16], P('rep', 'blk'), may hold values from 1 to 8, as said below
- grad_out: bfloat16 [98304, 128], P(('rep', 'blk')), may hold values from -6 to 6
Outputs:
- activations: bfloat16 [98304, 128], P(('rep', 'blk'))
- grad_weight: float32 [128, 128], replicated
- grad_features: bfloat16 [98304, 128], P(('rep', 'blk'))
Inputs may be any that keep to these rules, and one draw needn't show every extreme that they name: `tile_counts`: on every device some column block has all 8 slots live.
All inputs are finite; a program needn't handle non-finite values.
Results may differ from a plain program's by a relative error of at most 0.02.
Values may be sent and summed in bfloat16 or wider, within the bound.
No kernel may reach another device: no remote copies, remote signals or barrier semaphores. Data moves between devices by JAX's collectives and lax.ppermute only.
A program may use at most 64 MiB of HBM per device.

v0:
```python
import functools
import math

import jax
import jax.numpy as jnp
from jax import lax
from jax.experimental import pallas as pl
from jax.experimental.pallas import tpu as pltpu
from jax.sharding import Mesh, PartitionSpec as P

AXES = ("z_hi", "z_lo", "x_lo", "core", "y_hi", "y_lo", "x_hi")
Z = ("z_hi", "z_lo")
REP = ("z_hi", "z_lo", "x_lo", "core")
BLK = ("y_hi", "y_lo", "x_hi")
BF16 = jnp.bfloat16
F32 = jnp.float32
VMEM = pl.BlockSpec(memory_space=pltpu.VMEM)
SMEM = pl.BlockSpec(memory_space=pltpu.SMEM)
LIMIT = 24 * 1024 * 1024
FORWARD_LIMIT = 50 * 1024 * 1024
GROUP = 4


def chunk_of(pos, mine, z_count):
    return ((pos ^ mine) & 1) * (2 * z_count) + ((pos >> 1) & 3) * (z_count // 2) + (pos >> 3)


def forward_kernel(z_count, slots, mine_ref, pos_ref, counts_ref, tiles_ref, rows_ref, send_ref, keep_ref, acc_ref, held_ref, sems):
    blocks, tile, width = rows_ref.shape
    half = 2 * z_count
    mine = mine_ref[0]

    def fetch(j):
        part = pl.ds(j * slots, slots)
        return pltpu.make_async_copy(tiles_ref.at[part], held_ref.at[part], sems.at[j])

    def start_step(j, carry):
        fetch(j).start()
        return carry

    lax.fori_loop(0, blocks, start_step, 0)
    acc_ref[...] = jnp.zeros_like(acc_ref)

    def block_step(j):
        values = held_ref[pl.ds(j * slots, slots)].reshape(slots * tile, tile)
        product = jnp.dot(values, rows_ref[j], preferred_element_type=F32)
        count = counts_ref[0, 0, j]
        for s in range(slots):
            place = chunk_of(pos_ref[0, 0, j * slots + s], mine, z_count)
            place = jnp.where(s < count, place, 2 * half)
            acc_ref[place] += product[s * tile : (s + 1) * tile]

    def group_step(n, carry):
        for k in range(GROUP):
            fetch(n * GROUP + k).wait()
        for k in range(GROUP):
            block_step(n * GROUP + k)
        return carry

    lax.fori_loop(0, blocks // GROUP, group_step, 0)
    keep_ref[...] = acc_ref[0:half]
    send_ref[...] = acc_ref[half : 2 * half].astype(BF16)


def near_sum_kernel(parts_ref, out_ref):
    for z in range(out_ref.shape[0]):
        total = parts_ref[0, z].astype(F32)
        for n in range(1, parts_ref.shape[0]):
            total += parts_ref[n, z].astype(F32)
        out_ref[z] = total.astype(BF16)


def dense_kernel(parts_ref, weight_ref, bias_ref, grad_ref, act_ref, out_ref):
    tile = grad_ref.shape[0]
    total = parts_ref[0].astype(F32)
    for z in range(1, parts_ref.shape[0]):
        total += parts_ref[z].astype(F32)
    aggregate = total.astype(BF16)
    pre = jnp.dot(aggregate, weight_ref[...], preferred_element_type=F32) + bias_ref[...]
    low = jnp.exp(jnp.minimum(pre, 0.0))
    act_ref[...] = jnp.where(pre > 0, pre, low - 1.0).astype(BF16)
    slope = jnp.where(pre > 0, 1.0, low)
    grad_pre = (grad_ref[...].astype(F32) * slope).astype(BF16)
    out_ref[0:tile] = lax.dot_general(
        weight_ref[...], grad_pre, (((1,), (1,)), ((), ())), preferred_element_type=F32
    ).astype(BF16)
    out_ref[tile:] = lax.dot_general(
        aggregate, grad_pre, (((0,), (0,)), ((), ())), preferred_element_type=F32
    ).astype(BF16)


def column_block(slots, j, mine, pos_ref, counts_ref, tiles_ref, held_ref):
    count_of_places, tile, _ = held_ref.shape
    base = j * slots
    count = counts_ref[0, 0, j]
    picked = []
    for s in range(slots):
        place = chunk_of(pos_ref[0, 0, base + s], mine, count_of_places // 4)
        picked.append(held_ref[jnp.where(s < count, place, count_of_places - 1)])
    left = jnp.concatenate(picked, axis=1)
    values = tiles_ref[pl.ds(base, slots)].reshape(slots * tile, tile)
    return jnp.dot(left, values, preferred_element_type=F32)


def backward_kernel(
    slots, mine_ref, pos_ref, counts_ref, tiles_ref, own_ref, other_ref, out_ref, held_ref
):
    near_count, far_count, tile, _ = out_ref.shape
    far_count -= 1
    groups, each = own_ref.shape[0], own_ref.shape[1] - 1
    sums = []
    for n, ref in enumerate((own_ref, other_ref)):
        part = jnp.zeros((tile, tile), F32)
        for g in range(groups):
            held_ref[pl.ds((n * groups + g) * each, each)] = ref[g, 0:each]
            part += ref[g, each].astype(F32)
        sums.append(part)
    held_ref[2 * groups * each] = jnp.zeros((tile, tile), BF16)
    near, far = sums
    weight = (near + far).astype(BF16)
    for n in range(near_count):
        for m in range(far_count):
            out = column_block(slots, m * near_count + n, mine_ref[0], pos_ref, counts_ref, tiles_ref, held_ref)
            out_ref[n, m] = out.astype(BF16)
        out_ref[n, far_count] = weight


def pack_kernel(parts_ref, out_ref):
    far_count = out_ref.shape[0]
    tile = parts_ref.shape[2]

    def total(m):
        out = parts_ref[0, m].astype(F32)
        for n in range(1, parts_ref.shape[0]):
            out += parts_ref[n, m].astype(F32)
        return out.astype(BF16)

    weight = total(far_count)
    for m in range(far_count):
        out_ref[m, 0:tile] = total(m)
        out_ref[m, tile:] = weight


def finish_kernel(scale, parts_ref, grad_ref, weight_ref):
    tile = grad_ref.shape[0]
    total = parts_ref[0].astype(F32)
    for n in range(1, parts_ref.shape[0]):
        total += parts_ref[n].astype(F32)
    grad_ref[...] = total[0:tile].T.astype(BF16)
    weight_ref[...] = total[tile:] * scale


def shards(features, weight, bias, tile_vals, tile_pos, tile_counts, grad_out):
    z_count = lax.axis_size(Z)
    blocks = lax.axis_size(BLK)
    tile, width = features.shape
    tiles = tile_vals.reshape(tile_vals.shape[2:])
    slots = tiles.shape[0] // blocks
    nodes = tile * lax.axis_size(AXES)
    mine = (lax.axis_index("x_lo") * 2 + lax.axis_index("core")).astype(jnp.int32).reshape(1)
    params = pltpu.CompilerParams(vmem_limit_bytes=LIMIT)
    swap = [(0, 1), (1, 0)]
    features, mine = lax.optimization_barrier((features, mine))

    rows = lax.all_to_all(jnp.broadcast_to(features[None], (blocks, tile, width)), BLK, 0, 0, tiled=True)
    send, keep = pl.pallas_call(
        functools.partial(forward_kernel, z_count, slots),
        out_shape=(
            jax.ShapeDtypeStruct((2 * z_count, tile, width), BF16),
            jax.ShapeDtypeStruct((2 * z_count, tile, width), F32),
        ),
        in_specs=[SMEM, SMEM, SMEM, pl.BlockSpec(memory_space=pl.ANY), VMEM],
        out_specs=(VMEM, VMEM),
        scratch_shapes=[
            pltpu.VMEM((4 * z_count + 1, tile, width), F32),
            pltpu.VMEM(tiles.shape, BF16),
            pltpu.SemaphoreType.DMA((blocks,)),
        ],
        compiler_params=pltpu.CompilerParams(vmem_limit_bytes=FORWARD_LIMIT),
        name="forward",
    )(mine, tile_pos, tile_counts, tiles, rows)
    got = lax.ppermute(send, "core", swap)
    parts = (keep + got.astype(F32)).astype(BF16).reshape(4, z_count // 2, tile, width)
    parts = lax.all_to_all(parts, ("z_lo", "x_lo"), 0, 0, tiled=True)
    parts = pl.pallas_call(
        near_sum_kernel,
        out_shape=jax.ShapeDtypeStruct(parts.shape[1:], BF16),
        in_specs=[VMEM],
        out_specs=VMEM,
        compiler_params=params,
        name="near_sum",
    )(parts)
    parts = lax.all_to_all(parts, "z_hi", 0, 0, tiled=True)

    activations, packed = pl.pallas_call(
        dense_kernel,
        out_shape=(
            jax.ShapeDtypeStruct((tile, width), BF16),
            jax.ShapeDtypeStruct((2 * tile, width), BF16),
        ),
        in_specs=[VMEM] * 4,
        out_specs=(VMEM, VMEM),
        compiler_params=params,
        name="dense",
    )(parts, weight, bias.reshape(1, -1), grad_out)

    gathered = lax.all_gather(packed, "z_hi", axis=0)
    held = jnp.concatenate(
        [gathered[:, :tile], gathered[:, tile:].astype(F32).sum(0, keepdims=True).astype(BF16)], axis=0
    )
    own = lax.all_to_all(jnp.broadcast_to(held[None], (4, *held.shape)), ("z_lo", "x_lo"), 0, 0, tiled=True)
    other = lax.ppermute(own, "core", swap)
    near_count = lax.axis_size(("y_lo", "x_hi"))
    far_count = blocks // near_count
    chunks = pl.pallas_call(
        functools.partial(backward_kernel, slots),
        out_shape=jax.ShapeDtypeStruct((near_count, far_count + 1, tile, width), BF16),
        in_specs=[SMEM] * 3 + [VMEM] * 3,
        out_specs=VMEM,
        scratch_shapes=[pltpu.VMEM((4 * z_count + 1, tile, width), BF16)],
        compiler_params=params,
        name="backward",
    )(mine, tile_pos, tile_counts, tiles, own, other)
    parts = lax.all_to_all(chunks, ("y_lo", "x_hi"), 0, 0, tiled=True)
    chunks = pl.pallas_call(
        pack_kernel,
        out_shape=jax.ShapeDtypeStruct((far_count, 2 * tile, width), BF16),
        in_specs=[VMEM],
        out_specs=VMEM,
        compiler_params=params,
        name="pack",
    )(parts)
    parts = lax.all_to_all(chunks, "y_hi", 0, 0, tiled=True)
    grad_features, grad_weight = pl.pallas_call(
        functools.partial(finish_kernel, 1.0 / math.sqrt(nodes)),
        out_shape=(
            jax.ShapeDtypeStruct((tile, width), BF16),
            jax.ShapeDtypeStruct((width, width), F32),
        ),
        in_specs=[VMEM],
        out_specs=(VMEM, VMEM),
        compiler_params=params,
        name="finish",
    )(parts)
    return (activations, grad_weight, grad_features)


def solution(mesh):
    reps, blks = mesh.devices.shape
    fine = Mesh(mesh.devices.reshape(reps // 8, 2, 2, 2, blks // 4, 2, 2), AXES)
    in_specs = (
        P(AXES, None),
        P(),
        P(),
        P(REP, BLK, None, None, None),
        P(REP, BLK, None),
        P(REP, BLK, None),
        P(AXES, None),
    )
    out_specs = (P(AXES, None), P(), P(AXES, None))
    return jax.shard_map(shards, mesh=fine, in_specs=in_specs, out_specs=out_specs, check_vma=False)
```

profile of v0, /device:TPU:8, one launch (start us, length us, event | category | flops | bytes accessed | tf_op | source)
XLA Modules:
  0.0 149.4 jit_solution(12635598708806648811)
XLA Ops:
  0.6 0.0 copy-start.4
  0.6 0.0 copy-start.3
  0.7 0.9 broadcast_in_dim.4
  1.5 27.2 %all_to_all.30.rows_ref = bf16[16,128,128]{2,1,0:T(8,128)(2,1)S(1)} all-to-all(bf16[16,128,128]{2,1,0:T(8,128)(2,1)S(1)} %broadcast_in_dim.4), channel_id=1, replica_groups=mesh['z_hi'=6,'z_lo'=2,'x_lo'=2,'core'=2,'y_hi'=4,'y_lo'=2,'x_hi'=2] {'y..., dimensions={0} | all-to-all | bytes 1048576 | tf_op jit(solution)/shard_map/all_to_all | solution.py:165
  28.7 0.0 copy-done.4
  28.7 0.0 copy-done.3
  28.7 4.1 %forward.1 = (bf16[24,128,128]{2,1,0:T(8,128)(2,1)S(1)}, f32[24,128,128]{2,1,0:T(8,128)S(1)}) custom-call(s32[1]{0:T(128)} %bitcast.mine_ref, s32[1,1,128]{2,1,0:T(1,128)S(1)} %copy-done.3, s32[1,1,16]{2,1,0:T(1,128)S(1)} %copy-done.4, bf16[128,128,128]{2,1,0:T(8,128)(2,1)} %bitcast.6, bf16[16,128,128]{2,1,0:T(8,128)(2,1)S(1)} %all_to_all.30.rows_ref), custom_call_target="tpu_custom_call" | custom-call | tf_op jit(solution)/shard_map/forward/pallas_call | solution.py:166
  32.8 1.9 %collective-permute-start = (bf16[24,128,128]{2,1,0:T(8,128)(2,1)S(1)}, bf16[24,128,128]{2,1,0:T(8,128)(2,1)S(1)}, u32[]{:S(2)}, u32[]{:S(2)}) collective-permute-start(bf16[24,128,128]{2,1,0:T(8,128)(2,1)S(1)} %get-tuple-element.14), channel_id=1, source_target_pairs={{0,16},{16,0},{1,17},{17,1},{2,18},{18,2},{3,19},{19,3},{4,20},{20... | collective-permute-start | bytes 2359304 | tf_op jit(solution)/shard_map/ppermute | solution.py:182
  34.8 2.3 %collective-permute-done = bf16[24,128,128]{2,1,0:T(8,128)(2,1)S(1)} collective-permute-done((bf16[24,128,128]{2,1,0:T(8,128)(2,1)S(1)}, bf16[24,128,128]{2,1,0:T(8,128)(2,1)S(1)}, u32[]{:S(2)}, u32[]{:S(2)}) %collective-permute-start) | collective-permute-done | bytes 786464 | tf_op jit(solution)/shard_map/ppermute | solution.py:182
  37.0 0.2 add_convert_fusion
  37.2 0.0 copy-start.1
  37.3 0.0 copy-start.2
  37.3 0.0 copy-start.5
  37.3 14.5 %all_to_all.31.parts_ref = bf16[4,6,128,128]{3,2,1,0:T(8,128)(2,1)S(1)} all-to-all(bf16[4,6,128,128]{3,2,1,0:T(8,128)(2,1)S(1)} %bitcast.9), channel_id=1, replica_groups=mesh['z_hi'=6,'z_lo'=2,'x_lo'=2,'core'=2,'y_hi'=4,'y_lo'=2,'x_hi'=2] {'z..., dimensions={0} | all-to-all | bytes 1572864 | tf_op jit(solution)/shard_map/all_to_all | solution.py:184
  51.7 0.1 near_sum.1
  51.8 25.1 %all_to_all.32.parts_ref = bf16[6,128,128]{2,1,0:T(8,128)(2,1)S(1)} all-to-all(bf16[6,128,128]{2,1,0:T(8,128)(2,1)S(1)} %near_sum.1), channel_id=1, replica_groups=mesh['z_hi'=6,'z_lo'=2,'x_lo'=2,'core'=2,'y_hi'=4,'y_lo'=2,'x_hi'=2] {'z..., dimensions={0} | all-to-all | bytes 393216 | tf_op jit(solution)/shard_map/all_to_all | solution.py:193
  77.0 0.0 copy-done.1
  77.0 0.0 copy-done.2
  77.0 0.0 copy-done.5
  77.0 0.8 dense.1
  77.8 0.0 copy-start
  77.8 21.7 %all-gather = bf16[1536,128]{1,0:T(8,128)(2,1)S(1)} all-gather(bf16[256,128]{1,0:T(8,128)(2,1)S(1)} %get-tuple-element.16), channel_id=2, replica_groups=mesh['z_hi'=6,'z_lo'=2,'x_lo'=2,'core'=2,'y_hi'=4,'y_lo'=2,'x_hi'=2] {'z..., dimensions={0}, use_global_device_ids=true | all-gather | bytes 458752 | tf_op jit(solution)/shard_map/all_gather | solution.py:207
  99.5 0.2 broadcast_in_dim.5
  99.7 13.5 %all_to_all.33.own_ref = bf16[4,7,128,128]{3,2,1,0:T(8,128)(2,1)S(1)} all-to-all(bf16[4,7,128,128]{3,2,1,0:T(8,128)(2,1)S(1)} %broadcast_in_dim.5), channel_id=1, replica_groups=mesh['z_hi'=6,'z_lo'=2,'x_lo'=2,'core'=2,'y_hi'=4,'y_lo'=2,'x_hi'=2] {'z..., dimensions={0} | all-to-all | bytes 1835008 | tf_op jit(solution)/shard_map/all_to_all | solution.py:211
  113.2 1.9 %collective-permute-start.1 = (bf16[4,7,128,128]{3,2,1,0:T(8,128)(2,1)S(1)}, bf16[4,7,128,128]{3,2,1,0:T(8,128)(2,1)S(1)}, u32[]{:S(2)}, u32[]{:S(2)}) collective-permute-start(bf16[4,7,128,128]{3,2,1,0:T(8,128)(2,1)S(1)} %all_to_all.33.own_ref), channel_id=1, source_target_pairs={{0,16},{16,0},{1,17},{17,1},{2,18},{18,2},{3,19},{19,3},{4,20},{20... | collective-permute-start | bytes 2752520 | tf_op jit(solution)/shard_map/ppermute | solution.py:212
  115.1 2.4 %collective-permute-done.1.other_ref = bf16[4,7,128,128]{3,2,1,0:T(8,128)(2,1)S(1)} collective-permute-done((bf16[4,7,128,128]{3,2,1,0:T(8,128)(2,1)S(1)}, bf16[4,7,128,128]{3,2,1,0:T(8,128)(2,1)S(1)}, u32[]{:S(2)}, u32[]{:S(2)}) %collective-permute-start.1) | collective-permute-done | bytes 917536 | tf_op jit(solution)/shard_map/ppermute | solution.py:212
  117.6 0.0 copy-done
  117.6 2.0 %backward.1 = bf16[4,5,128,128]{3,2,1,0:T(8,128)(2,1)S(1)} custom-call(s32[1]{0:T(128)} %bitcast.mine_ref, s32[1,1,128]{2,1,0:T(1,128)S(1)} %copy-done.3, s32[1,1,16]{2,1,0:T(1,128)S(1)} %copy-done.4, bf16[128,128,128]{2,1,0:T(8,128)(2,1)S(1)} %bitcast.7, bf16[4,7,128,128]{3,2,1,0:T(8,128)(2,1)S(1)} %all_to_all.33.own_ref, ...), custom_call_target="tpu_custom_call" | custom-call | tf_op jit(solution)/shard_map/backward/pallas_call | solution.py:215
  119.6 15.5 %all_to_all.34.parts_ref = bf16[4,5,128,128]{3,2,1,0:T(8,128)(2,1)S(1)} all-to-all(bf16[4,5,128,128]{3,2,1,0:T(8,128)(2,1)S(1)} %backward.1), channel_id=1, replica_groups=mesh['z_hi'=6,'z_lo'=2,'x_lo'=2,'core'=2,'y_hi'=4,'y_lo'=2,'x_hi'=2] {'y..., dimensions={0} | all-to-all | bytes 1310720 | tf_op jit(solution)/shard_map/all_to_all | solution.py:224
  135.1 0.1 pack.1
  135.2 13.5 %all_to_all.35.parts_ref = bf16[4,256,128]{2,1,0:T(8,128)(2,1)S(1)} all-to-all(bf16[4,256,128]{2,1,0:T(8,128)(2,1)S(1)} %pack.1), channel_id=1, replica_groups=mesh['z_hi'=6,'z_lo'=2,'x_lo'=2,'core'=2,'y_hi'=4,'y_lo'=2,'x_hi'=2] {'y..., dimensions={0} | all-to-all | bytes 524288 | tf_op jit(solution)/shard_map/all_to_all | solution.py:233
  148.6 0.7 finish.1
  (2 shorter events, 0.1 us)
Async XLA Ops:
  0.6 28.1 %copy-start.4 = (s32[1,1,16]{2,1,0:T(1,128)S(1)}, s32[1,1,16]{2,1,0:T(1,128)}, u32[]{:S(2)}) copy-start(s32[1,1,16]{2,1,0:T(1,128)} %counts_ref.3) | copy-start | bytes 196
  0.6 28.1 %copy-start.3 = (s32[1,1,128]{2,1,0:T(1,128)S(1)}, s32[1,1,128]{2,1,0:T(1,128)}, u32[]{:S(2)}) copy-start(s32[1,1,128]{2,1,0:T(1,128)} %pos_ref.3) | copy-start | bytes 1540
  32.8 4.2 %collective-permute-start = (bf16[24,128,128]{2,1,0:T(8,128)(2,1)S(1)}, bf16[24,128,128]{2,1,0:T(8,128)(2,1)S(1)}, u32[]{:S(2)}, u32[]{:S(2)}) collective-permute-start(bf16[24,128,128]{2,1,0:T(8,128)(2,1)S(1)} %get-tuple-element.14), channel_id=1, source_target_pairs={{0,16},{16,0},{1,17},{17,1},{2,18},{18,2},{3,19},{19,3},{4,20},{20... | collective-permute-start | bytes 2359304 | tf_op jit(solution)/shard_map/ppermute | solution.py:182
  37.2 39.7 %copy-start.1 = (bf16[128,128]{1,0:T(8,128)(2,1)S(1)}, bf16[128,128]{1,0:T(8,128)(2,1)}, u32[]{:S(2)}) copy-start(bf16[128,128]{1,0:T(8,128)(2,1)} %weight_ref.1) | copy-start | bytes 98308
  37.3 39.7 %copy-start.2 = (bf16[128,128]{1,0:T(8,128)(2,1)S(1)}, bf16[128,128]{1,0:T(8,128)(2,1)}, u32[]{:S(2)}) copy-start(bf16[128,128]{1,0:T(8,128)(2,1)} %grad_ref.1) | copy-start | bytes 98308
  37.3 39.7 %copy-start.5 = (f32[128]{0:T(128)S(1)}, f32[128]{0:T(128)}, u32[]{:S(2)}) copy-start(f32[128]{0:T(128)} %param.9) | copy-start | bytes 1540
  77.8 39.8 %copy-start = (bf16[1,1,128,128,128]{4,3,2,1,0:T(8,128)(2,1)S(1)}, bf16[1,1,128,128,128]{4,3,2,1,0:T(8,128)(2,1)}, u32[]{:S(2)}) copy-start(bf16[1,1,128,128,128]{4,3,2,1,0:T(8,128)(2,1)} %param.10) | copy-start | bytes 12582916
  113.2 4.4 %collective-permute-start.1 = (bf16[4,7,128,128]{3,2,1,0:T(8,128)(2,1)S(1)}, bf16[4,7,128,128]{3,2,1,0:T(8,128)(2,1)S(1)}, u32[]{:S(2)}, u32[]{:S(2)}) collective-permute-start(bf16[4,7,128,128]{3,2,1,0:T(8,128)(2,1)S(1)} %all_to_all.33.own_ref), channel_id=1, source_target_pairs={{0,16},{16,0},{1,17},{17,1},{2,18},{18,2},{3,19},{19,3},{4,20},{20... | collective-permute-start | bytes 2752520 | tf_op jit(solution)/shard_map/ppermute | solution.py:212
where the time goes:
time: 150 us; the launch traced here: 149 us
  blocking collectives  131 us (87%)
  Pallas kernels  7.81 us (5%)
  waiting for transfers between devices  4.69 us (3%)
  starting transfers between devices  3.83 us (3%)
    all_to_all x1, blocking collectives, shards(): lax.all_to_all(jnp.broadcast_to(features[None], (blocks, tile, width)), B...  27.2 us
    all_to_all x1, blocking collectives, shards(): parts = lax.all_to_all(parts, 'z_hi', 0, 0, tiled=True)  25.1 us
    all_gather x1, blocking collectives, shards(): gathered = lax.all_gather(packed, 'z_hi', axis=0)  21.7 us
    all_to_all x1, blocking collectives, shards(): parts = lax.all_to_all(chunks, ('y_lo', 'x_hi'), 0, 0, tiled=True)  15.5 us
    all_to_all x1, blocking collectives, shards(): parts = lax.all_to_all(parts, ('z_lo', 'x_lo'), 0, 0, tiled=True)  14.5 us
    all_to_all x1, blocking collectives, shards(): parts = lax.all_to_all(chunks, 'y_hi', 0, 0, tiled=True)  13.5 us
    all_to_all x1, blocking collectives, shards(): lax.all_to_all(jnp.broadcast_to(held[None], (4, *held.shape)), ('z_lo', '...  13.5 us
    pallas_call x1, Pallas kernels, shards(): pl.pallas_call(functools.partial(forward_kernel, z_count, slots), out_sha...  4.12 us
  transfers between devices with their start and end apart: 2, of which 2 were waited for; matrix products, arithmetic and copies ran while one was open for 0% of the time, Pallas kernels for 0%

commit v1 on v0

--- a/solution.py
+++ b/solution.py
@@ -26,7 +26,8 @@
 
 
 def forward_kernel(z_count, slots, mine_ref, pos_ref, counts_ref, tiles_ref, rows_ref, send_ref, keep_ref, acc_ref, held_ref, sems):
-    blocks, tile, width = rows_ref.shape
+    near_count, far_count, tile, width = rows_ref.shape
+    blocks = near_count * far_count
     half = 2 * z_count
     mine = mine_ref[0]
 
@@ -43,7 +44,7 @@
 
     def block_step(j):
         values = held_ref[pl.ds(j * slots, slots)].reshape(slots * tile, tile)
-        product = jnp.dot(values, rows_ref[j], preferred_element_type=F32)
+        product = jnp.dot(values, rows_ref[j % near_count, j // near_count], preferred_element_type=F32)
         count = counts_ref[0, 0, j]
         for s in range(slots):
             place = chunk_of(pos_ref[0, 0, j * slots + s], mine, z_count)
@@ -162,7 +163,11 @@
     swap = [(0, 1), (1, 0)]
     features, mine = lax.optimization_barrier((features, mine))
 
-    rows = lax.all_to_all(jnp.broadcast_to(features[None], (blocks, tile, width)), BLK, 0, 0, tiled=True)
+    near_count = lax.axis_size(("y_lo", "x_hi"))
+    far_count = blocks // near_count
+    rows = lax.all_to_all(jnp.broadcast_to(features[None], (far_count, tile, width)), "y_hi", 0, 0, tiled=True)
+    rows = jnp.broadcast_to(rows[None], (near_count, far_count, tile, width))
+    rows = lax.all_to_all(rows, ("y_lo", "x_hi"), 0, 0, tiled=True)
     send, keep = pl.pallas_call(
         functools.partial(forward_kernel, z_count, slots),
         out_shape=(
@@ -210,8 +215,6 @@
     )
     own = lax.all_to_all(jnp.broadcast_to(held[None], (4, *held.shape)), ("z_lo", "x_lo"), 0, 0, tiled=True)
     other = lax.ppermute(own, "core", swap)
-    near_count = lax.axis_size(("y_lo", "x_hi"))
-    far_count = blocks // near_count
     chunks = pl.pallas_call(
         functools.partial(backward_kernel, slots),
         out_shape=jax.ShapeDtypeStruct((near_count, far_count + 1, tile, width), BF16),

time: 150 us -> 151 us (level)
  the two profiles are of different devices: /device:TPU:8 before, /device:TPU:2 now
where the time goes in v1:
time: 151 us; the launch traced here: 150 us
  blocking collectives  132 us (87%)
  Pallas kernels  7.78 us (5%)
  waiting for transfers between devices  4.69 us (3%)
  starting transfers between devices  3.83 us (3%)
    all_to_all x1, blocking collectives, shards(): parts = lax.all_to_all(parts, 'z_hi', 0, 0, tiled=True)  24.3 us
    all_gather x1, blocking collectives, shards(): gathered = lax.all_gather(packed, 'z_hi', axis=0)  21.8 us
    all_to_all x1, blocking collectives, shards(): parts = lax.all_to_all(parts, ('z_lo', 'x_lo'), 0, 0, tiled=True)  17.1 us
    all_to_all x1, blocking collectives, shards(): lax.all_to_all(jnp.broadcast_to(features[None], (far_count, tile, width))...  15.8 us
    all_to_all x1, blocking collectives, shards(): parts = lax.all_to_all(chunks, ('y_lo', 'x_hi'), 0, 0, tiled=True)  14.4 us
    all_to_all x1, blocking collectives, shards(): parts = lax.all_to_all(chunks, 'y_hi', 0, 0, tiled=True)  13.2 us
    all_to_all x1, blocking collectives, shards(): lax.all_to_all(jnp.broadcast_to(held[None], (4, *held.shape)), ('z_lo', '...  12.6 us
    all_to_all x1, blocking collectives, shards(): rows = lax.all_to_all(rows, ('y_lo', 'x_hi'), 0, 0, tiled=True)  12.2 us
  transfers between devices with their start and end apart: 2, of which 2 were waited for; matrix products, arithmetic and copies ran while one was open for 0% of the time, Pallas kernels for 0%

profile of v1, /device:TPU:2, one launch (start us, length us, event | category | flops | bytes accessed | tf_op | source)
XLA Modules:
  0.0 150.0 jit_solution(6699676888610170576)
XLA Ops:
  0.6 0.0 copy-start.4
  0.6 0.0 copy-start.3
  0.7 0.8 broadcast_in_dim.6
  1.4 15.8 %all_to_all.35 = bf16[4,128,128]{2,1,0:T(8,128)(2,1)S(1)} all-to-all(bf16[4,128,128]{2,1,0:T(8,128)(2,1)S(1)} %broadcast_in_dim.6), channel_id=1, replica_groups=mesh['z_hi'=6,'z_lo'=2,'x_lo'=2,'core'=2,'y_hi'=4,'y_lo'=2,'x_hi'=2] {'y..., dimensions={0} | all-to-all | bytes 262144 | tf_op jit(solution)/shard_map/all_to_all | solution.py:168
  17.3 0.1 broadcast_in_dim.7
  17.4 12.2 %all_to_all.36.rows_ref = bf16[4,4,128,128]{3,2,1,0:T(8,128)(2,1)S(1)} all-to-all(bf16[4,4,128,128]{3,2,1,0:T(8,128)(2,1)S(1)} %broadcast_in_dim.7), channel_id=1, replica_groups=mesh['z_hi'=6,'z_lo'=2,'x_lo'=2,'core'=2,'y_hi'=4,'y_lo'=2,'x_hi'=2] {'y..., dimensions={0} | all-to-all | bytes 1048576 | tf_op jit(solution)/shard_map/all_to_all | solution.py:170
  29.6 0.0 copy-done.4
  29.6 0.0 copy-done.3
  29.6 4.1 %forward.1 = (bf16[24,128,128]{2,1,0:T(8,128)(2,1)S(1)}, f32[24,128,128]{2,1,0:T(8,128)S(1)}) custom-call(s32[1]{0:T(128)} %bitcast.mine_ref, s32[1,1,128]{2,1,0:T(1,128)S(1)} %copy-done.3, s32[1,1,16]{2,1,0:T(1,128)S(1)} %copy-done.4, bf16[128,128,128]{2,1,0:T(8,128)(2,1)} %bitcast.6, bf16[4,4,128,128]{3,2,1,0:T(8,128)(2,1)S(1)} %all_to_all.36.rows_ref), custom_call_target="tpu_custom_call" | custom-call | tf_op jit(solution)/shard_map/forward/pallas_call | solution.py:171
  33.7 1.9 %collective-permute-start = (bf16[24,128,128]{2,1,0:T(8,128)(2,1)S(1)}, bf16[24,128,128]{2,1,0:T(8,128)(2,1)S(1)}, u32[]{:S(2)}, u32[]{:S(2)}) collective-permute-start(bf16[24,128,128]{2,1,0:T(8,128)(2,1)S(1)} %get-tuple-element.14), channel_id=1, source_target_pairs={{0,16},{16,0},{1,17},{17,1},{2,18},{18,2},{3,19},{19,3},{4,20},{20... | collective-permute-start | bytes 2359304 | tf_op jit(solution)/shard_map/ppermute | solution.py:187
  35.6 2.3 %collective-permute-done = bf16[24,128,128]{2,1,0:T(8,128)(2,1)S(1)} collective-permute-done((bf16[24,128,128]{2,1,0:T(8,128)(2,1)S(1)}, bf16[24,128,128]{2,1,0:T(8,128)(2,1)S(1)}, u32[]{:S(2)}, u32[]{:S(2)}) %collective-permute-start) | collective-permute-done | bytes 786464 | tf_op jit(solution)/shard_map/ppermute | solution.py:187
  37.9 0.2 add_convert_fusion
  38.1 0.0 copy-start.1
  38.1 0.0 copy-start.2
  38.1 0.0 copy-start.5
  38.1 17.1 %all_to_all.37.parts_ref = bf16[4,6,128,128]{3,2,1,0:T(8,128)(2,1)S(1)} all-to-all(bf16[4,6,128,128]{3,2,1,0:T(8,128)(2,1)S(1)} %bitcast.9), channel_id=1, replica_groups=mesh['z_hi'=6,'z_lo'=2,'x_lo'=2,'core'=2,'y_hi'=4,'y_lo'=2,'x_hi'=2] {'z..., dimensions={0} | all-to-all | bytes 1572864 | tf_op jit(solution)/shard_map/all_to_all | solution.py:189
  55.3 0.1 near_sum.1
  55.4 24.3 %all_to_all.38.parts_ref = bf16[6,128,128]{2,1,0:T(8,128)(2,1)S(1)} all-to-all(bf16[6,128,128]{2,1,0:T(8,128)(2,1)S(1)} %near_sum.1), channel_id=1, replica_groups=mesh['z_hi'=6,'z_lo'=2,'x_lo'=2,'core'=2,'y_hi'=4,'y_lo'=2,'x_hi'=2] {'z..., dimensions={0} | all-to-all | bytes 393216 | tf_op jit(solution)/shard_map/all_to_all | solution.py:198
  79.6 0.0 copy-done.1
  79.6 0.0 copy-done.2
  79.6 0.0 copy-done.5
  79.6 0.8 dense.1
  80.4 0.0 copy-start
  80.4 21.8 %all-gather = bf16[1536,128]{1,0:T(8,128)(2,1)S(1)} all-gather(bf16[256,128]{1,0:T(8,128)(2,1)S(1)} %get-tuple-element.16), channel_id=2, replica_groups=mesh['z_hi'=6,'z_lo'=2,'x_lo'=2,'core'=2,'y_hi'=4,'y_lo'=2,'x_hi'=2] {'z..., dimensions={0}, use_global_device_ids=true | all-gather | bytes 458752 | tf_op jit(solution)/shard_map/all_gather | solution.py:212
  102.3 0.2 broadcast_in_dim.8
  102.5 12.6 %all_to_all.39.own_ref = bf16[4,7,128,128]{3,2,1,0:T(8,128)(2,1)S(1)} all-to-all(bf16[4,7,128,128]{3,2,1,0:T(8,128)(2,1)S(1)} %broadcast_in_dim.8), channel_id=1, replica_groups=mesh['z_hi'=6,'z_lo'=2,'x_lo'=2,'core'=2,'y_hi'=4,'y_lo'=2,'x_hi'=2] {'z..., dimensions={0} | all-to-all | bytes 1835008 | tf_op jit(solution)/shard_map/all_to_all | solution.py:216
  115.2 1.9 %collective-permute-start.1 = (bf16[4,7,128,128]{3,2,1,0:T(8,128)(2,1)S(1)}, bf16[4,7,128,128]{3,2,1,0:T(8,128)(2,1)S(1)}, u32[]{:S(2)}, u32[]{:S(2)}) collective-permute-start(bf16[4,7,128,128]{3,2,1,0:T(8,128)(2,1)S(1)} %all_to_all.39.own_ref), channel_id=1, source_target_pairs={{0,16},{16,0},{1,17},{17,1},{2,18},{18,2},{3,19},{19,3},{4,20},{20... | collective-permute-start | bytes 2752520 | tf_op jit(solution)/shard_map/ppermute | solution.py:217
  117.1 2.4 %collective-permute-done.1.other_ref = bf16[4,7,128,128]{3,2,1,0:T(8,128)(2,1)S(1)} collective-permute-done((bf16[4,7,128,128]{3,2,1,0:T(8,128)(2,1)S(1)}, bf16[4,7,128,128]{3,2,1,0:T(8,128)(2,1)S(1)}, u32[]{:S(2)}, u32[]{:S(2)}) %collective-permute-start.1) | collective-permute-done | bytes 917536 | tf_op jit(solution)/shard_map/ppermute | solution.py:217
  119.5 0.0 copy-done
  119.5 2.0 %backward.1 = bf16[4,5,128,128]{3,2,1,0:T(8,128)(2,1)S(1)} custom-call(s32[1]{0:T(128)} %bitcast.mine_ref, s32[1,1,128]{2,1,0:T(1,128)S(1)} %copy-done.3, s32[1,1,16]{2,1,0:T(1,128)S(1)} %copy-done.4, bf16[128,128,128]{2,1,0:T(8,128)(2,1)S(1)} %bitcast.7, bf16[4,7,128,128]{3,2,1,0:T(8,128)(2,1)S(1)} %all_to_all.39.own_ref, ...), custom_call_target="tpu_custom_call" | custom-call | tf_op jit(solution)/shard_map/backward/pallas_call | solution.py:218
  121.5 14.4 %all_to_all.40.parts_ref = bf16[4,5,128,128]{3,2,1,0:T(8,128)(2,1)S(1)} all-to-all(bf16[4,5,128,128]{3,2,1,0:T(8,128)(2,1)S(1)} %backward.1), channel_id=1, replica_groups=mesh['z_hi'=6,'z_lo'=2,'x_lo'=2,'core'=2,'y_hi'=4,'y_lo'=2,'x_hi'=2] {'y..., dimensions={0} | all-to-all | bytes 1310720 | tf_op jit(solution)/shard_map/all_to_all | solution.py:227
  135.9 0.1 pack.1
  136.0 13.2 %all_to_all.41.parts_ref = bf16[4,256,128]{2,1,0:T(8,128)(2,1)S(1)} all-to-all(bf16[4,256,128]{2,1,0:T(8,128)(2,1)S(1)} %pack.1), channel_id=1, replica_groups=mesh['z_hi'=6,'z_lo'=2,'x_lo'=2,'core'=2,'y_hi'=4,'y_lo'=2,'x_hi'=2] {'y..., dimensions={0} | all-to-all | bytes 524288 | tf_op jit(solution)/shard_map/all_to_all | solution.py:236
  149.2 0.7 finish.1
  (2 shorter events, 0.1 us)
Async XLA Ops:
  0.6 28.9 %copy-start.4 = (s32[1,1,16]{2,1,0:T(1,128)S(1)}, s32[1,1,16]{2,1,0:T(1,128)}, u32[]{:S(2)}) copy-start(s32[1,1,16]{2,1,0:T(1,128)} %counts_ref.3) | copy-start | bytes 196
  0.6 28.9 %copy-start.3 = (s32[1,1,128]{2,1,0:T(1,128)S(1)}, s32[1,1,128]{2,1,0:T(1,128)}, u32[]{:S(2)}) copy-start(s32[1,1,128]{2,1,0:T(1,128)} %pos_ref.3) | copy-start | bytes 1540
  33.7 4.2 %collective-permute-start = (bf16[24,128,128]{2,1,0:T(8,128)(2,1)S(1)}, bf16[24,128,128]{2,1,0:T(8,128)(2,1)S(1)}, u32[]{:S(2)}, u32[]{:S(2)}) collective-permute-start(bf16[24,128,128]{2,1,0:T(8,128)(2,1)S(1)} %get-tuple-element.14), channel_id=1, source_target_pairs={{0,16},{16,0},{1,17},{17,1},{2,18},{18,2},{3,19},{19,3},{4,20},{20... | collective-permute-start | bytes 2359304 | tf_op jit(solution)/shard_map/ppermute | solution.py:187
  38.1 41.6 %copy-start.1 = (bf16[128,128]{1,0:T(8,128)(2,1)S(1)}, bf16[128,128]{1,0:T(8,128)(2,1)}, u32[]{:S(2)}) copy-start(bf16[128,128]{1,0:T(8,128)(2,1)} %weight_ref.1) | copy-start | bytes 98308
  38.1 41.5 %copy-start.2 = (bf16[128,128]{1,0:T(8,128)(2,1)S(1)}, bf16[128,128]{1,0:T(8,128)(2,1)}, u32[]{:S(2)}) copy-start(bf16[128,128]{1,0:T(8,128)(2,1)} %grad_ref.1) | copy-start | bytes 98308
  38.1 41.5 %copy-start.5 = (f32[128]{0:T(128)S(1)}, f32[128]{0:T(128)}, u32[]{:S(2)}) copy-start(f32[128]{0:T(128)} %param.9) | copy-start | bytes 1540
  80.4 39.1 %copy-start = (bf16[1,1,128,128,128]{4,3,2,1,0:T(8,128)(2,1)S(1)}, bf16[1,1,128,128,128]{4,3,2,1,0:T(8,128)(2,1)}, u32[]{:S(2)}) copy-start(bf16[1,1,128,128,128]{4,3,2,1,0:T(8,128)(2,1)} %param.10) | copy-start | bytes 12582916
  115.2 4.4 %collective-permute-start.1 = (bf16[4,7,128,128]{3,2,1,0:T(8,128)(2,1)S(1)}, bf16[4,7,128,128]{3,2,1,0:T(8,128)(2,1)S(1)}, u32[]{:S(2)}, u32[]{:S(2)}) collective-permute-start(bf16[4,7,128,128]{3,2,1,0:T(8,128)(2,1)S(1)} %all_to_all.39.own_ref), channel_id=1, source_target_pairs={{0,16},{16,0},{1,17},{17,1},{2,18},{18,2},{3,19},{19,3},{4,20},{20... | collective-permute-start | bytes 2752520 | tf_op jit(solution)/shard_map/ppermute | solution.py:217
